TPU v7x, 512 devices: a whole 4x8x8 slice. The times are simulated.
512 devices in a mesh: rec: 16 (over z, core), frame: 32 (over x, y).
Axes of the slice: x: 4, y: 8, z: 8, core: 2. Of those that a mesh axis runs over, the one named last changes fastest.
Arguments:
- frames: bfloat16 [16, 49152, 256], P('rec', 'frame'), may hold values from -10 to 10
- texts: bfloat16 [32, 224, 256], P('rec', 'frame'), may hold values from -100 to 100
- pair_rec: int32 [32, 1], replicated, may hold values from 0 to 15, as said below
- pair_text: int32 [32], replicated, may hold values from 0 to 31, as said below
- pair_label: int32 [32], replicated, may hold values 0 or 1
Outputs:
- loss: float32 [], replicated
- grad_frames: bfloat16 [16, 49152, 256], P('rec', 'frame')
- grad_texts: bfloat16 [32, 224, 256], P('rec', 'frame')
Inputs may be any that keep to these rules, and one draw needn't show every extreme that they name: `pair_rec`: no recording is named by more than 6 pairs, some recording by exactly 6, and every recording by at least one. A pair's text is held by the index of rec one after, one before, or 8 after its recording (counted round): pair_text // 2 = (pair_rec + k) mod 16 with k one of 1, 15, 8.
All inputs are finite; a program needn't handle non-finite values.
Results may differ from a plain program's by a relative error of at most 0.0085.
Values may be sent and summed in bfloat16 or wider, within the bound.
A program may use at most 64 MiB of HBM per device.

v0:
```python
import jax
import jax.numpy as jnp
from jax import lax
from jax.sharding import PartitionSpec as P

MOST = 6
EPS = 1e-06
TEMP = 10.0
BIAS = -1.0
LOSS_SCALE = 2048.0


def slot_tables(pair_rec, pair_text, pair_label, here, most):
    record = pair_rec[:, 0]
    count = record.shape[0]
    order = jnp.arange(count, dtype=jnp.int32)
    same = (record[:, None] == record[None, :]).astype(jnp.int32)
    earlier = (order[None, :] < order[:, None]).astype(jnp.int32)
    rank = jnp.sum(same * earlier, axis=1)
    places = jnp.arange(most, dtype=jnp.int32)
    chosen = ((record[None, :] == here) & (rank[None, :] == places[:, None])).astype(jnp.int32)
    valid = jnp.sum(chosen, axis=1)
    slot_text = jnp.sum(chosen * pair_text[None, :], axis=1)
    sign = jnp.sum(chosen * (2 * pair_label[None, :] - 1), axis=1)
    return (valid, slot_text, sign)


def pair_terms(score, valid, sign, tokens):
    margin = -sign * (TEMP * score + BIAS)
    loss_part = valid * jax.nn.softplus(margin)
    grad_cos = -LOSS_SCALE * TEMP * valid * sign * jax.nn.sigmoid(margin) / tokens
    return (loss_part, grad_cos)


def body(frames, texts, pair_rec, pair_text, pair_label):
    here = lax.axis_index("rec")
    part = lax.axis_index("frame")
    owned, width_rows, width = texts.shape
    tokens = width_rows * lax.axis_size("frame")
    n_text = owned * lax.axis_size("rec")
    valid, slot_text, sign = slot_tables(pair_rec, pair_text, pair_label, here, MOST)
    valid_f = valid.astype(jnp.float32)
    sign_f = sign.astype(jnp.float32)
    picks = (
        (slot_text[:, None] == jnp.arange(n_text, dtype=jnp.int32)[None, :]) & (valid[:, None] > 0)
    ).astype(jnp.bfloat16)
    whole = lax.all_gather(texts, "frame", axis=1, tiled=True)
    query_vectors = jnp.einsum(
        "jc,cgx->jgx",
        picks,
        lax.all_gather(whole, "rec", axis=0, tiled=True),
        preferred_element_type=jnp.float32,
    ).astype(jnp.bfloat16)
    upstream_signal = frames[0]
    logit_scale = width ** (-0.5)
    pair_scores = (
        jnp.einsum(
            "ype,je->ypj", query_vectors, upstream_signal, preferred_element_type=jnp.float32
        )
        * logit_scale
    )
    local_max = jnp.max(pair_scores, axis=2)
    row_max = lax.pmax(local_max, "frame")
    expo = jnp.exp(pair_scores - row_max[..., None])
    batch_weights = expo.astype(jnp.bfloat16)
    value_partial = jnp.einsum(
        "pqx,xh->pqh", batch_weights, upstream_signal, preferred_element_type=jnp.float32
    )
    query_f = query_vectors.astype(jnp.float32)
    q_norm = lax.rsqrt(jnp.sum(query_f * query_f, axis=2) + EPS)
    q_unit = query_f * q_norm[..., None]
    context = lax.psum(value_partial, "frame")
    c_norm = lax.rsqrt(jnp.sum(context * context, axis=2) + EPS)
    c_unit = context * c_norm[..., None]
    cos = jnp.sum(q_unit * c_unit, axis=2)
    score = jnp.mean(cos, axis=1)
    loss_part, grad_cos = pair_terms(score, valid_f, sign_f, tokens)
    weight = grad_cos[:, None, None]
    d_context = weight * (q_unit - cos[..., None] * c_unit) * c_norm[..., None]
    direct = weight * (c_unit - cos[..., None] * q_unit) * q_norm[..., None]
    direct_own = lax.dynamic_slice_in_dim(direct, part * width_rows, width_rows, 1)
    context_batch_gradient = d_context.astype(jnp.bfloat16)
    weight_gradient = jnp.einsum(
        "ype,je->ypj", context_batch_gradient, upstream_signal, preferred_element_type=jnp.float32
    )
    score_gradient = (expo * weight_gradient * logit_scale).astype(jnp.bfloat16)
    d_query = lax.psum_scatter(
        jnp.einsum(
            "slf,fd->lsd", score_gradient, upstream_signal, preferred_element_type=jnp.float32
        ),
        "frame",
        scatter_dimension=0,
        tiled=True,
    )
    d_query = d_query + jnp.transpose(direct_own, (1, 0, 2))
    text_term = jnp.einsum(
        "st,lsd->tld", picks.astype(jnp.float32), d_query, precision=lax.Precision.HIGHEST
    )
    grad_texts = lax.psum_scatter(text_term, "rec", scatter_dimension=0, tiled=True).astype(
        jnp.bfloat16
    )
    frame_loss_piece = jnp.einsum(
        "cvm,cvz->mz", score_gradient, query_vectors, preferred_element_type=jnp.float32
    )
    frame_loss_piece = frame_loss_piece + jnp.einsum(
        "cvm,cvz->mz", batch_weights, context_batch_gradient, preferred_element_type=jnp.float32
    )
    grad_frames = frame_loss_piece.astype(jnp.bfloat16)[None]
    loss = lax.psum(jnp.sum(loss_part), "rec")
    return (loss, grad_frames, grad_texts)


def solution(mesh):
    return jax.shard_map(
        body,
        mesh=mesh,
        in_specs=(P("rec", "frame", None), P("rec", "frame", None), P(), P(), P()),
        out_specs=(P(), P("rec", "frame", None), P("rec", "frame", None)),
        check_vma=False,
    )
```

profile of v0, /device:TPU:16, one launch (start us, length us, event | category | flops | bytes accessed | tf_op | source)
XLA Modules:
  0.0 644.4 jit_solution(15901261809968272552)
XLA Ops:
  7.2 49.8 %all_gather.6 = bf16[2,224,256]{2,0,1:T(2,128)(2,1)S(1)} all-gather(bf16[2,7,256]{2,0,1:T(2,128)(2,1)} %param.6), channel_id=1, replica_groups=mesh['rec'=16,'frame'=32] {'frame'}, dimensions={1}, use_global_device_ids=true | all-gather | bytes 236544 | tf_op jit(solution)/shard_map/all_gather | solution.py:47
  57.0 0.7 copy.20
  57.8 0.9 select_reduce_fusion
  58.7 0.7 broadcast_compare_fusion.1
  59.4 0.7 multiply_add_fusion
  60.1 1.3 select_reduce_fusion.2
  61.4 43.4 %all-gather.2.cloned.1.call-done = bf16[32,224,256]{2,1,0:T(8,128)(2,1)} async-done(((bf16[2,224,256]{2,1,0:T(8,128)(2,1)}), bf16[32,224,256]{2,1,0:T(8,128)(2,1)}) %all-gather.2.cloned.1.call-update) | async-done | bytes 3670032 | tf_op jit(solution)/shard_map/all_gather | solution.py:51
  104.7 4.3 fusion.6
  109.0 4.4 multiply_reduce_fusion
  113.4 71.4 %pmax.7 = f32[6,224]{1,0:T(8,128)S(1)} all-reduce(f32[6,224]{1,0:T(8,128)S(1)} %get-tuple-element.17), channel_id=1, replica_groups=mesh['rec'=16,'frame'=32] {'frame'}, use_global_device_ids=true, to_apply=%region_6.0 | all-reduce | flops 1344 | bytes 10752 | tf_op jit(solution)/shard_map/pmax | solution.py:63
  184.8 4.9 fusion.13
  189.7 2.1 copy.23
  191.8 0.2 reduce-scatter.3.cloned.1.call-start
  192.0 0.7 add_rsqrt_fusion.1
  192.6 157.1 %all-reduce.5.cloned.1.call-done = f32[6,224,256]{2,0,1:T(8,128)} async-done(((f32[6,224,256]{2,0,1:T(8,128)}), f32[6,224,256]{2,0,1:T(8,128)}) %all-reduce.5.cloned.1.call-update) | async-done | bytes 1376272 | tf_op jit(solution)/shard_map/psum | solution.py:72
  349.7 1.9 multiply_reduce_fusion.1
  351.6 2.4 multiply_reduce_fusion.2
  354.0 1.4 fusion.44
  355.4 1.8 convert_multiply_fusion
  357.2 4.9 multiply_convert_fusion
  362.2 1.3 fusion.10
  363.5 0.7 copy-done.10
  364.2 2.1 copy.47
  366.2 1.3 dynamic-slice
  368.2 0.7 constant_dynamic-slice_fusion
  368.9 0.7 constant_dynamic-slice_fusion.1
  369.6 5.7 convolution_bitcast_fusion
  375.3 2.3 fusion.5
  377.6 209.2 %reduce-scatter.3.cloned.1.call-done = f32[7,6,256]{2,1,0:T(8,128)} async-done(((f32[224,6,256]{2,1,0:T(8,128)}), f32[7,6,256]{2,1,0:T(8,128)}) %reduce-scatter.3.cloned.1.call-update) | async-done | bytes 43024 | tf_op jit(solution)/shard_map/reduce_scatter | solution.py:87
  586.9 1.3 fusion.27
  588.2 49.1 %all-reduce.6 = (f32[]{:T(128)}, bf16[32,7,256]{2,0,1:T(8,128)(2,1)S(1)}) all-reduce(f32[]{:T(128)} %get-tuple-element.14, f32[32,7,256]{2,0,1:T(8,128)S(1)} %fusion.27), channel_id=1, replica_groups=mesh['rec'=16,'frame'=32] {'rec'}, use_global_device_ids=true, to_apply=%region_11.12 | all-reduce | flops 57345 | bytes 344072 | tf_op jit(solution)/shard_map/psum | solution.py:109
  637.3 0.6 dynamic-slice_convert_fusion
  (30 shorter events, 0.2 us)
Async XLA Ops:
  7.2 101.8 %copy-start = (bf16[1,1536,256]{2,1,0:T(8,128)(2,1)S(1)}, bf16[1,1536,256]{2,1,0:T(8,128)(2,1)}, u32[]{:S(2)}) copy-start(bf16[1,1536,256]{2,1,0:T(8,128)(2,1)} %param.5) | copy-start | bytes 2359300
  7.2 97.5 %all-gather.2.cloned.1.call-start = ((), (), s32[]{:S(2)}) async-start(), calls=%async_computation.1 | async-start | bytes 3899392 | tf_op jit(solution)/shard_map/all_gather | solution.py:51
  57.8 291.9 %all-reduce.5.cloned.1.call-start = ((), (), s32[]{:S(2)}) async-start(), calls=%async_computation.2 | async-start | bytes 3670016 | tf_op jit(solution)/shard_map/psum | solution.py:72
  61.3 43.4 %copy-start.9 = (s32[6]{0:T(128)}, s32[6]{0:T(128)S(1)}, u32[]{:S(2)}) copy-start(s32[6]{0:T(128)S(1)} %get-tuple-element.7) | copy-start | bytes 76
  61.3 47.6 %copy-start.4 = (s32[6]{0:T(128)}, s32[6]{0:T(128)S(1)}, u32[]{:S(2)}) copy-start(s32[6]{0:T(128)S(1)} %get-tuple-element.6) | copy-start | bytes 76
  61.4 47.6 %copy-start.8 = (pred[6]{0:T(512)(128)(4,1)}, pred[6]{0:T(512)(128)(4,1)S(1)}, u32[]{:S(2)}) copy-start(pred[6]{0:T(512)(128)(4,1)S(1)} %broadcast_compare_fusion) | copy-start | bytes 22
  191.8 395.1 %reduce-scatter.3.cloned.1.call-start = ((), (), s32[]{:S(2)}) async-start(), calls=%async_computation.3 | async-start | bytes 1892352 | tf_op jit(solution)/shard_map/reduce_scatter | solution.py:87
  349.7 5.7 copy-start.1
  354.0 3.2 copy-start.3
  355.4 6.8 %copy-start.6 = (f32[6]{0:T(128)}, f32[6]{0:T(128)S(1)}, u32[]{:S(2)}) copy-start(f32[6]{0:T(128)S(1)} %get-tuple-element.13) | copy-start | bytes 76
  357.2 5.0 copy-start.2
  362.2 2.0 copy-start.10
  369.6 5.7 copy-start.11
  375.3 211.6 %copy-start.5 = (s32[6]{0:T(128)S(1)}, s32[6]{0:T(128)}, u32[]{:S(2)}) copy-start(s32[6]{0:T(128)} %copy-done.4) | copy-start | bytes 76
  375.3 211.6 %copy-start.7 = (f32[6]{0:T(128)S(1)}, f32[6]{0:T(128)}, u32[]{:S(2)}) copy-start(f32[6]{0:T(128)} %copy-done.6) | copy-start | bytes 76
Sparse Core Ops, SparseCore 0:
  57.9 46.7 all-gather.1
  191.9 157.7 all-reduce.4
  366.4 220.4 reduce-scatter.2
where the time goes:
time: 645 us; the launch traced here: 644 us
  waiting for transfers between devices  410 us (64%)
  blocking collectives  170 us (26%)
  matrix products  29 us (4%)
  between operations  14.6 us (2%)
  other arithmetic  11.7 us (2%)
  local copies, waits for them, and re-layouts  8.88 us (1%)
    reduce_scatter x1, waiting for transfers between devices, body(): lax.psum_scatter(jnp.einsum('slf,fd->lsd', score_gradient, upstream_signa...  209 us
    psum x1, waiting for transfers between devices, body(): context = lax.psum(value_partial, 'frame')  157 us
    pmax x1, blocking collectives, body(): row_max = lax.pmax(local_max, 'frame')  71.4 us
    all_gather x1, blocking collectives, body(): whole = lax.all_gather(texts, 'frame', axis=1, tiled=True)  49.8 us
    psum x1, blocking collectives, body(): loss = lax.psum(jnp.sum(loss_part), 'rec')  49.1 us
    all_gather x1, waiting for transfers between devices, body(): lax.all_gather(whole, 'rec', axis=0, tiled=True)  43.4 us
  transfers between devices with their start and end apart: 3, of which 3 were waited for; matrix products, arithmetic and copies ran while one was open for 2% of the time, Pallas kernels for 0%

commit v1 on v0

--- a/solution.py
+++ b/solution.py
@@ -45,11 +45,35 @@
         (slot_text[:, None] == jnp.arange(n_text, dtype=jnp.int32)[None, :]) & (valid[:, None] > 0)
     ).astype(jnp.bfloat16)
     whole = lax.all_gather(texts, "frame", axis=1, tiled=True)
-    query_vectors = jnp.einsum(
-        "jc,cgx->jgx",
-        picks,
-        lax.all_gather(whole, "rec", axis=0, tiled=True),
-        preferred_element_type=jnp.float32,
+
+    def ticks_manage(shard_in, link_axis, local):
+        v1 = lax.psum(1, link_axis)
+        res = lax.axis_index(link_axis)
+        now, q_next, carry = (v1, res, shard_in.shape[0])
+        pages = [(k, (k + 1) % now) for k in range(now)]
+        leaves = [(k, (k - 1) % now) for k in range(now)]
+        response = now // 2
+        o_now = reached = shard_in
+        block_now = local(shard_in, q_next * carry)
+        for ii in [*range(1, response + 1)]:
+            o_now = lax.ppermute(o_now, link_axis, pages)
+            if ii < now - response:
+                reached = lax.ppermute(reached, link_axis, leaves)
+                odd = local(reached, (q_next + ii) % now * carry)
+                block_now = block_now + odd
+            p_next = local(o_now, (q_next - ii) % now * carry)
+            block_now = block_now + p_next
+        return block_now
+
+    query_vectors = ticks_manage(
+        whole,
+        "rec",
+        lambda part_2, offset: jnp.einsum(
+            "jc,cgx->jgx",
+            lax.dynamic_slice_in_dim(picks, offset, part_2.shape[0], axis=1),
+            part_2,
+            preferred_element_type=jnp.float32,
+        ),
     ).astype(jnp.bfloat16)
     upstream_signal = frames[0]
     logit_scale = width ** (-0.5)

time: 645 us -> 656 us (1.017)
  waiting for transfers between devices: 410 us -> 386 us
  starting transfers between devices: 0.3 us -> 24.2 us
  matrix products: 29 us -> 42.9 us
    all_gather x1 -> x0, waiting for transfers between devices: 43.4 us -> none  [body(): lax.all_gather(whole, 'rec', axis=0, tiled=True)]
    ppermute x0 -> x15, starting transfers between devices: none -> 24.1 us  [the longest x7 24.1 us: ticks_manage(): reached = lax.ppermute(reached, link_axis, leaves)]
    ppermute x0 -> x15, waiting for transfers between devices: none -> 16.9 us  [the longest x8 16.8 us: ticks_manage(): o_now = lax.ppermute(o_now, link_axis, pages)]
    dot_general x1 -> x16, matrix products: 4.25 us -> 18.3 us  [body(): jnp.einsum('jc,cgx->jgx', lax.dynamic_slice_in_dim(picks, offset, part_2....]
  transfers between devices with their start and end apart: 3 -> 17, of which waited for: 3 -> 9; matrix products, arithmetic and copies ran while one was open for 2% -> 4% of each run, Pallas kernels for 0% -> 0%
where the time goes in v1:
time: 656 us; the launch traced here: 655 us
  waiting for transfers between devices  386 us (59%)
  blocking collectives  168 us (26%)
  matrix products  42.9 us (7%)
  starting transfers between devices  24.2 us (4%)
  between operations  15.1 us (2%)
  other arithmetic  9.81 us (1%)
  local copies, waits for them, and re-layouts  8.82 us (1%)
    reduce_scatter x1, waiting for transfers between devices, body(): lax.psum_scatter(jnp.einsum('slf,fd->lsd', score_gradient, upstream_signa...  209 us
    psum x1, waiting for transfers between devices, body(): context = lax.psum(value_partial, 'frame')  160 us
    pmax x1, blocking collectives, body(): row_max = lax.pmax(local_max, 'frame')  69.5 us
    all_gather x1, blocking collectives, body(): whole = lax.all_gather(texts, 'frame', axis=1, tiled=True)  49.8 us
    psum x1, blocking collectives, body(): loss = lax.psum(jnp.sum(loss_part), 'rec')  49.1 us
    ppermute x7, starting transfers between devices, ticks_manage(): reached = lax.ppermute(reached, link_axis, leaves)  24.1 us
    dot_general x16, matrix products, body(): jnp.einsum('jc,cgx->jgx', lax.dynamic_slice_in_dim(picks, offset, part_2....  18.3 us
    ppermute x8, waiting for transfers between devices, ticks_manage(): o_now = lax.ppermute(o_now, link_axis, pages)  16.8 us
  transfers between devices with their start and end apart: 17, of which 9 were waited for; matrix products, arithmetic and copies ran while one was open for 4% of the time, Pallas kernels for 0%

profile of v1, /device:TPU:16, one launch (start us, length us, event | category | flops | bytes accessed | tf_op | source)
XLA Modules:
  0.0 655.5 jit_solution(12194371327748313545)
XLA Ops:
  7.2 49.8 %all_gather.3 = bf16[2,224,256]{2,0,1:T(2,128)(2,1)S(1)} all-gather(bf16[2,7,256]{2,0,1:T(2,128)(2,1)} %param.6), channel_id=1, replica_groups=mesh['rec'=16,'frame'=32] {'frame'}, dimensions={1}, use_global_device_ids=true | all-gather | bytes 236544 | tf_op jit(solution)/shard_map/all_gather | solution.py:47
  57.0 2.9 collective-permute-start
  64.7 6.2 collective-permute-start.2
  71.9 2.7 collective-permute-done.3
  74.6 3.0 collective-permute-start.4
  78.5 2.7 collective-permute-done.5
  81.2 3.0 collective-permute-start.6
  85.2 2.7 collective-permute-done.7
  87.9 3.0 collective-permute-start.8
  91.8 2.7 collective-permute-done.9
  94.5 3.0 collective-permute-start.10
  98.5 2.7 collective-permute-done.11
  101.2 3.0 collective-permute-start.12
  104.2 1.7 fusion.68
  105.9 1.7 fusion.65
  107.9 1.7 fusion.74
  109.6 1.7 fusion.71
  111.3 3.2 collective-permute-done.14
  114.5 6.0 fusion.4
  120.6 4.5 multiply_reduce_fusion
  125.0 69.5 %pmax.7 = f32[6,224]{1,0:T(8,128)S(1)} all-reduce(f32[6,224]{1,0:T(8,128)S(1)} %get-tuple-element.17), channel_id=1, replica_groups=mesh['rec'=16,'frame'=32] {'frame'}, use_global_device_ids=true, to_apply=%region_6.7 | all-reduce | flops 1344 | bytes 10752 | tf_op jit(solution)/shard_map/pmax | solution.py:87
  194.5 4.9 fusion.8
  199.4 2.1 copy.21
  202.2 160.2 %all-reduce.5.cloned.1.call-done = f32[6,224,256]{2,0,1:T(8,128)} async-done(((f32[6,224,256]{2,0,1:T(8,128)}), f32[6,224,256]{2,0,1:T(8,128)}) %all-reduce.5.cloned.1.call-update) | async-done | bytes 1376272 | tf_op jit(solution)/shard_map/psum | solution.py:96
  362.4 2.0 multiply_reduce_fusion.1
  366.3 1.8 convert_multiply_fusion
  368.1 5.0 multiply_convert_fusion
  375.0 2.1 copy.42
  380.6 5.7 convolution_bitcast_fusion
  386.3 2.3 fusion.3
  388.6 209.1 %reduce-scatter.3.cloned.1.call-done = f32[7,6,256]{2,1,0:T(8,128)} async-done(((f32[224,6,256]{2,1,0:T(8,128)}), f32[7,6,256]{2,1,0:T(8,128)}) %reduce-scatter.3.cloned.1.call-update) | async-done | bytes 43024 | tf_op jit(solution)/shard_map/reduce_scatter | solution.py:111
  598.9 49.1 %all-reduce.6 = (f32[]{:T(128)}, bf16[32,7,256]{2,0,1:T(8,128)(2,1)S(1)}) all-reduce(f32[]{:T(128)} %get-tuple-element.14, f32[32,7,256]{2,0,1:T(8,128)S(1)} %fusion.22), channel_id=1, replica_groups=mesh['rec'=16,'frame'=32] {'rec'}, use_global_device_ids=true, to_apply=%region_11.12 | all-reduce | flops 57345 | bytes 344072 | tf_op jit(solution)/shard_map/psum | solution.py:133
  (80 shorter events, 18.8 us)
Async XLA Ops:
  7.2 113.4 %copy-start = (bf16[1,1536,256]{2,1,0:T(8,128)(2,1)S(1)}, bf16[1,1536,256]{2,1,0:T(8,128)(2,1)}, u32[]{:S(2)}) copy-start(bf16[1,1536,256]{2,1,0:T(8,128)(2,1)} %param.5) | copy-start | bytes 2359300
  7.2 355.2 %all-reduce.5.cloned.1.call-start = ((), (), s32[]{:S(2)}) async-start(), calls=%async_computation.1 | async-start | bytes 3670016 | tf_op jit(solution)/shard_map/psum | solution.py:96
  57.0 7.6 %collective-permute-start.1 = (bf16[2,224,256]{2,0,1:T(2,128)(2,1)S(1)}, bf16[2,224,256]{2,0,1:T(2,128)(2,1)S(1)}, u32[]{:S(2)}, u32[]{:S(2)}) collective-permute-start(bf16[2,224,256]{2,0,1:T(2,128)(2,1)S(1)} %all_gather.3), channel_id=1, source_target_pairs={{0,32},{32,64},{64,96},{96,128},{128,160},{160,192},{192,224},{224... | collective-permute-start | bytes 688136 | tf_op jit(solution)/shard_map/ppermute | solution.py:59
  57.0 7.6 %collective-permute-start = (bf16[2,224,256]{2,0,1:T(2,128)(2,1)S(1)}, bf16[2,224,256]{2,0,1:T(2,128)(2,1)S(1)}, u32[]{:S(2)}, u32[]{:S(2)}) collective-permute-start(bf16[2,224,256]{2,0,1:T(2,128)(2,1)S(1)} %all_gather.3), channel_id=1, source_target_pairs={{0,480},{32,0},{64,32},{96,64},{128,96},{160,128},{192,160},{224,1... | collective-permute-start | bytes 688136 | tf_op jit(solution)/shard_map/ppermute | solution.py:61
  63.5 7.9 %copy-start.8 = (s32[6]{0:T(128)}, s32[6]{0:T(128)S(1)}, u32[]{:S(2)}) copy-start(s32[6]{0:T(128)S(1)} %get-tuple-element.6) | copy-start | bytes 76
  64.0 7.4 %copy-start.10 = (pred[6]{0:T(512)(128)(4,1)}, pred[6]{0:T(512)(128)(4,1)S(1)}, u32[]{:S(2)}) copy-start(pred[6]{0:T(512)(128)(4,1)S(1)} %broadcast_compare_fusion) | copy-start | bytes 22
  64.6 9.9 %collective-permute-start.3 = (bf16[2,224,256]{2,0,1:T(2,128)(2,1)S(1)}, bf16[2,224,256]{2,0,1:T(2,128)(2,1)S(1)}, u32[]{:S(2)}, u32[]{:S(2)}) collective-permute-start(bf16[2,224,256]{2,0,1:T(2,128)(2,1)S(1)} %collective-permute-done.1), channel_id=1, source_target_pairs={{0,32},{32,64},{64,96},{96,128},{128,160},{160,192},{192,224},{224... | collective-permute-start | bytes 688136 | tf_op jit(solution)/shard_map/ppermute | solution.py:59
  64.7 9.9 %collective-permute-start.2 = (bf16[2,224,256]{2,0,1:T(2,128)(2,1)S(1)}, bf16[2,224,256]{2,0,1:T(2,128)(2,1)S(1)}, u32[]{:S(2)}, u32[]{:S(2)}) collective-permute-start(bf16[2,224,256]{2,0,1:T(2,128)(2,1)S(1)} %collective-permute-done), channel_id=1, source_target_pairs={{0,480},{32,0},{64,32},{96,64},{128,96},{160,128},{192,160},{224,1... | collective-permute-start | bytes 688136 | tf_op jit(solution)/shard_map/ppermute | solution.py:61
  74.6 6.7 %collective-permute-start.5 = (bf16[2,224,256]{2,0,1:T(2,128)(2,1)S(1)}, bf16[2,224,256]{2,0,1:T(2,128)(2,1)S(1)}, u32[]{:S(2)}, u32[]{:S(2)}) collective-permute-start(bf16[2,224,256]{2,0,1:T(2,128)(2,1)S(1)} %collective-permute-done.3), channel_id=1, source_target_pairs={{0,32},{32,64},{64,96},{96,128},{128,160},{160,192},{192,224},{224... | collective-permute-start | bytes 688136 | tf_op jit(solution)/shard_map/ppermute | solution.py:59
  74.6 6.7 %collective-permute-start.4 = (bf16[2,224,256]{2,0,1:T(2,128)(2,1)S(1)}, bf16[2,224,256]{2,0,1:T(2,128)(2,1)S(1)}, u32[]{:S(2)}, u32[]{:S(2)}) collective-permute-start(bf16[2,224,256]{2,0,1:T(2,128)(2,1)S(1)} %collective-permute-done.2), channel_id=1, source_target_pairs={{0,480},{32,0},{64,32},{96,64},{128,96},{160,128},{192,160},{224,1... | collective-permute-start | bytes 688136 | tf_op jit(solution)/shard_map/ppermute | solution.py:61
  81.2 6.7 %collective-permute-start.7 = (bf16[2,224,256]{2,0,1:T(2,128)(2,1)S(1)}, bf16[2,224,256]{2,0,1:T(2,128)(2,1)S(1)}, u32[]{:S(2)}, u32[]{:S(2)}) collective-permute-start(bf16[2,224,256]{2,0,1:T(2,128)(2,1)S(1)} %collective-permute-done.5), channel_id=1, source_target_pairs={{0,32},{32,64},{64,96},{96,128},{128,160},{160,192},{192,224},{224... | collective-permute-start | bytes 688136 | tf_op jit(solution)/shard_map/ppermute | solution.py:59
  81.2 6.7 %collective-permute-start.6 = (bf16[2,224,256]{2,0,1:T(2,128)(2,1)S(1)}, bf16[2,224,256]{2,0,1:T(2,128)(2,1)S(1)}, u32[]{:S(2)}, u32[]{:S(2)}) collective-permute-start(bf16[2,224,256]{2,0,1:T(2,128)(2,1)S(1)} %collective-permute-done.4), channel_id=1, source_target_pairs={{0,480},{32,0},{64,32},{96,64},{128,96},{160,128},{192,160},{224,1... | collective-permute-start | bytes 688136 | tf_op jit(solution)/shard_map/ppermute | solution.py:61
  87.9 6.7 %collective-permute-start.9 = (bf16[2,224,256]{2,0,1:T(2,128)(2,1)S(1)}, bf16[2,224,256]{2,0,1:T(2,128)(2,1)S(1)}, u32[]{:S(2)}, u32[]{:S(2)}) collective-permute-start(bf16[2,224,256]{2,0,1:T(2,128)(2,1)S(1)} %collective-permute-done.7), channel_id=1, source_target_pairs={{0,32},{32,64},{64,96},{96,128},{128,160},{160,192},{192,224},{224... | collective-permute-start | bytes 688136 | tf_op jit(solution)/shard_map/ppermute | solution.py:59
  87.9 6.7 %collective-permute-start.8 = (bf16[2,224,256]{2,0,1:T(2,128)(2,1)S(1)}, bf16[2,224,256]{2,0,1:T(2,128)(2,1)S(1)}, u32[]{:S(2)}, u32[]{:S(2)}) collective-permute-start(bf16[2,224,256]{2,0,1:T(2,128)(2,1)S(1)} %collective-permute-done.6), channel_id=1, source_target_pairs={{0,480},{32,0},{64,32},{96,64},{128,96},{160,128},{192,160},{224,1... | collective-permute-start | bytes 688136 | tf_op jit(solution)/shard_map/ppermute | solution.py:61
  94.5 6.7 %collective-permute-start.11 = (bf16[2,224,256]{2,0,1:T(2,128)(2,1)S(1)}, bf16[2,224,256]{2,0,1:T(2,128)(2,1)S(1)}, u32[]{:S(2)}, u32[]{:S(2)}) collective-permute-start(bf16[2,224,256]{2,0,1:T(2,128)(2,1)S(1)} %collective-permute-done.9), channel_id=1, source_target_pairs={{0,32},{32,64},{64,96},{96,128},{128,160},{160,192},{192,224},{224... | collective-permute-start | bytes 688136 | tf_op jit(solution)/shard_map/ppermute | solution.py:59
  94.5 6.7 %collective-permute-start.10 = (bf16[2,224,256]{2,0,1:T(2,128)(2,1)S(1)}, bf16[2,224,256]{2,0,1:T(2,128)(2,1)S(1)}, u32[]{:S(2)}, u32[]{:S(2)}) collective-permute-start(bf16[2,224,256]{2,0,1:T(2,128)(2,1)S(1)} %collective-permute-done.8), channel_id=1, source_target_pairs={{0,480},{32,0},{64,32},{96,64},{128,96},{160,128},{192,160},{224,1... | collective-permute-start | bytes 688136 | tf_op jit(solution)/shard_map/ppermute | solution.py:61
  101.2 6.7 %collective-permute-start.13 = (bf16[2,224,256]{2,0,1:T(2,128)(2,1)S(1)}, bf16[2,224,256]{2,0,1:T(2,128)(2,1)S(1)}, u32[]{:S(2)}, u32[]{:S(2)}) collective-permute-start(bf16[2,224,256]{2,0,1:T(2,128)(2,1)S(1)} %collective-permute-done.11), channel_id=1, source_target_pairs={{0,32},{32,64},{64,96},{96,128},{128,160},{160,192},{192,224},{224... | collective-permute-start | bytes 688136 | tf_op jit(solution)/shard_map/ppermute | solution.py:59
  101.2 8.4 %collective-permute-start.12 = (bf16[2,224,256]{2,0,1:T(2,128)(2,1)S(1)}, bf16[2,224,256]{2,0,1:T(2,128)(2,1)S(1)}, u32[]{:S(2)}, u32[]{:S(2)}) collective-permute-start(bf16[2,224,256]{2,0,1:T(2,128)(2,1)S(1)} %collective-permute-done.10), channel_id=1, source_target_pairs={{0,480},{32,0},{64,32},{96,64},{128,96},{160,128},{192,160},{224,1... | collective-permute-start | bytes 688136 | tf_op jit(solution)/shard_map/ppermute | solution.py:61
  107.9 6.7 %collective-permute-start.14 = (bf16[2,224,256]{2,0,1:T(2,128)(2,1)S(1)}, bf16[2,224,256]{2,0,1:T(2,128)(2,1)S(1)}, u32[]{:S(2)}, u32[]{:S(2)}) collective-permute-start(bf16[2,224,256]{2,0,1:T(2,128)(2,1)S(1)} %collective-permute-done.13), channel_id=1, source_target_pairs={{0,32},{32,64},{64,96},{96,128},{128,160},{160,192},{192,224},{224... | collective-permute-start | bytes 688136 | tf_op jit(solution)/shard_map/ppermute | solution.py:59
  199.4 2.2 copy-start.5
  201.5 396.2 %reduce-scatter.3.cloned.1.call-start = ((), (), s32[]{:S(2)}) async-start(), calls=%async_computation.2 | async-start | bytes 1892352 | tf_op jit(solution)/shard_map/reduce_scatter | solution.py:111
  362.4 2.1 copy-start.1
  362.4 2.1 copy-start.2
  364.4 1.2 copy-start.11
  364.4 1.2 copy-start.13
  365.6 2.4 copy-start.4
  366.3 1.8 copy-start.6
  368.1 5.0 copy-start.3
  373.1 2.0 copy-start.14
  380.6 5.7 copy-start.15
  386.3 211.5 %copy-start.7 = (f32[6]{0:T(128)S(1)}, f32[6]{0:T(128)}, u32[]{:S(2)}) copy-start(f32[6]{0:T(128)} %copy-done.6) | copy-start | bytes 76
  386.3 211.5 %copy-start.9 = (s32[6]{0:T(128)S(1)}, s32[6]{0:T(128)}, u32[]{:S(2)}) copy-start(s32[6]{0:T(128)} %copy-done.8) | copy-start | bytes 76
  (1 other events, 0.5 us)
Sparse Core Ops, SparseCore 0:
  201.6 160.7 all-reduce.4
  377.2 220.4 reduce-scatter.2
